TPU v7x, 32 devices: a whole 2x2x4 slice. The times are simulated.
32 devices in a mesh: path: 8 (over z, x), fsdp: 4 (over y, core).
Axes of the slice: x: 2, y: 2, z: 4, core: 2. Of those that a mesh axis runs over, the one named last changes fastest.
Arguments:
- hidden_in: bfloat16 [8, 512, 1024], P('path', 'fsdp'), may hold values from -40 to 40
- cotangent: bfloat16 [8, 512, 1024], P('path', 'fsdp'), may hold values from -6 to 6
- up_weight: bfloat16 [8, 1024, 4096], P(None, 'path', 'fsdp'), may hold values from -4 to 4
- down_weight: bfloat16 [8, 1024, 4096], P(None, 'path', 'fsdp'), may hold values from -4 to 4
- up_moment: bfloat16 [8, 1024, 4096], P(None, 'path', 'fsdp'), may hold values from -3 to 3
- down_moment: bfloat16 [8, 1024, 4096], P(None, 'path', 'fsdp'), may hold values from -3 to 3
- sharing: int32 [8, 2], replicated, may hold values from 0 to 7, as said below
Outputs:
- new_up: bfloat16 [8, 1024, 4096], P(None, 'path', 'fsdp')
- new_down: bfloat16 [8, 1024, 4096], P(None, 'path', 'fsdp')
- new_up_moment: bfloat16 [8, 1024, 4096], P(None, 'path', 'fsdp')
- new_down_moment: bfloat16 [8, 1024, 4096], P(None, 'path', 'fsdp')
Inputs may be any that keep to these rules, and one draw needn't show every extreme that they name: `sharing`: column 0 names a first-level module, 0 to 3; column 1 a second-level module, 4 to 7. Every module is named by at least one path.
All inputs are finite; a program needn't handle non-finite values.
Results may differ from a plain program's by a relative error of at most 0.014.
Values may be sent and summed in bfloat16 or wider, within the bound.
A program may use at most 128 MiB of HBM per device.

v0:
```python
import math

import jax
import jax.numpy as jnp
from jax import lax
from jax.sharding import PartitionSpec as P

inner_rate = 2.0
outer_rate = 0.7
keep_rate = 0.9
norm_eps = 1e-06
tanh_coeff = 0.7978845608028654
cube_coeff = 0.044715


def gelu_value(values):
    inside = tanh_coeff * (values + cube_coeff * values * values * values)
    return 0.5 * values * (1.0 + jnp.tanh(inside))


def gelu_slope(values):
    inside = tanh_coeff * (values + cube_coeff * values * values * values)
    tangent = jnp.tanh(inside)
    return 0.5 * (1.0 + tangent) + 0.5 * values * (1.0 - tangent * tangent) * tanh_coeff * (
        1.0 + 3.0 * cube_coeff * values * values
    )


def row_scale(values):
    return lax.rsqrt(jnp.mean(values * values, axis=-1, keepdims=True) + norm_eps)


def gather_rows(values):
    return lax.all_gather(values, "fsdp", axis=0, tiled=True)


def whole_sum(values):
    return lax.psum(values, "fsdp")


def against_rows(left, right, factor):
    return (
        lax.dot_general(left, right, (((1,), (1,)), ((), ())), preferred_element_type=jnp.float32)
        * factor
    )


def over_rows(left, right, factor):
    return (
        lax.dot_general(left, right, (((0,), (0,)), ((), ())), preferred_element_type=jnp.float32)
        * factor
    )


def second_module(normed_all, cot_all, up_second, down_second, in_scale, hid_scale):
    pre_second = jnp.dot(normed_all, up_second, preferred_element_type=jnp.float32) * in_scale
    hidden_second = gelu_value(pre_second).astype(jnp.bfloat16)
    back_hidden = jnp.dot(cot_all, down_second, preferred_element_type=jnp.float32) * hid_scale
    grad_down = over_rows(cot_all, hidden_second, hid_scale)
    back_pre = (back_hidden * gelu_slope(pre_second)).astype(jnp.bfloat16)
    grad_up = over_rows(normed_all, back_pre, in_scale)
    return (back_pre, grad_up, grad_down)


def norm_back(cot_vals, scale_second, unit_second, back_normed):
    centred = back_normed - unit_second * jnp.mean(
        back_normed * unit_second, axis=-1, keepdims=True
    )
    return (cot_vals + scale_second * centred).astype(jnp.bfloat16)


def outer_step(weight, moment, mean_delta):
    new_moment = keep_rate * moment.astype(jnp.float32) + mean_delta
    new_weight = weight.astype(jnp.float32) - outer_rate * (mean_delta + keep_rate * new_moment)
    return (new_weight.astype(jnp.bfloat16), new_moment.astype(jnp.bfloat16))


def body(hidden_in, cotangent, up_weight, down_weight, up_moment, down_moment, sharing):
    tokens_own = hidden_in[0].astype(jnp.float32)
    cot_own = cotangent[0]
    module_count, piece_rows, piece_cols = up_weight.shape
    path_count = lax.axis_size("path")
    depth = piece_rows * path_count
    width = piece_cols * lax.axis_size("fsdp")
    in_scale = 1.0 / math.sqrt(depth)
    hid_scale = 1.0 / math.sqrt(width)
    row_count = tokens_own.shape[0]
    chosen = jnp.transpose(sharing)
    send_up = jnp.take(up_weight, chosen, axis=0)
    send_down = jnp.take(down_weight, chosen, axis=0)
    fetched_up, fetched_down = (
        lax.all_to_all(send_up, "path", split_axis=1, concat_axis=1, tiled=True),
        lax.all_to_all(send_down, "path", split_axis=1, concat_axis=1, tiled=True),
    )
    fetched_up = fetched_up.reshape(2, depth, piece_cols)
    fetched_down = fetched_down.reshape(2, depth, piece_cols)
    up_first, up_second = (fetched_up[0], fetched_up[1])
    down_first, down_second = (fetched_down[0], fetched_down[1])
    normed_first = (tokens_own * row_scale(tokens_own)).astype(jnp.bfloat16)
    normed_first_all = gather_rows(normed_first)
    cot_all = gather_rows(cot_own)
    pre_first = jnp.dot(normed_first_all, up_first, preferred_element_type=jnp.float32) * in_scale
    hidden_first = gelu_value(pre_first).astype(jnp.bfloat16)
    offset = lax.axis_index("fsdp") * row_count
    branch_term = against_rows(hidden_first, down_first, hid_scale)
    own_block = lax.dynamic_slice_in_dim(branch_term, offset, row_count, 0) + tokens_own
    middle_all = whole_sum(lax.dynamic_update_slice_in_dim(branch_term, own_block, offset, 0))
    scale_all = row_scale(middle_all)
    unit_all = middle_all * scale_all
    back_pre, grad_up_second, grad_down_second = second_module(
        unit_all.astype(jnp.bfloat16), cot_all, up_second, down_second, in_scale, hid_scale
    )
    back_normed_all = whole_sum(against_rows(back_pre, up_second, in_scale))
    back_middle_all = norm_back(cot_all.astype(jnp.float32), scale_all, unit_all, back_normed_all)
    back_hidden_first = (
        jnp.dot(back_middle_all, down_first, preferred_element_type=jnp.float32) * hid_scale
    )
    grad_down_first = over_rows(back_middle_all, hidden_first, hid_scale)
    back_pre_first = (back_hidden_first * gelu_slope(pre_first)).astype(jnp.bfloat16)
    grad_up_first = over_rows(normed_first_all, back_pre_first, in_scale)
    delta_up = (inner_rate * jnp.stack([grad_up_first, grad_up_second])).astype(jnp.bfloat16)
    delta_down = (inner_rate * jnp.stack([grad_down_first, grad_down_second])).astype(jnp.bfloat16)
    delta_up = delta_up.reshape(2, path_count, piece_rows, piece_cols)
    delta_down = delta_down.reshape(2, path_count, piece_rows, piece_cols)
    came_up, came_down = (
        lax.all_to_all(delta_up, "path", split_axis=1, concat_axis=1, tiled=True),
        lax.all_to_all(delta_down, "path", split_axis=1, concat_axis=1, tiled=True),
    )
    flat_up = came_up.reshape(2 * path_count, piece_rows * piece_cols)
    flat_down = came_down.reshape(2 * path_count, piece_rows * piece_cols)
    owners = chosen.reshape(-1)
    member = owners[None, :] == jnp.arange(module_count, dtype=jnp.int32)[:, None]
    counts = jnp.sum(member.astype(jnp.float32), axis=1)
    member_mat = member.astype(jnp.bfloat16)
    mean_up = (
        jnp.dot(member_mat, flat_up, preferred_element_type=jnp.float32) / counts[:, None]
    ).reshape(module_count, piece_rows, piece_cols)
    mean_down = (
        jnp.dot(member_mat, flat_down, preferred_element_type=jnp.float32) / counts[:, None]
    ).reshape(module_count, piece_rows, piece_cols)
    new_up, new_up_moment = outer_step(up_weight, up_moment, mean_up)
    new_down, new_down_moment = outer_step(down_weight, down_moment, mean_down)
    return (new_up, new_down, new_up_moment, new_down_moment)


def solution(mesh):
    in_specs = (
        P("path", "fsdp", None),
        P("path", "fsdp", None),
        P(None, "path", "fsdp"),
        P(None, "path", "fsdp"),
        P(None, "path", "fsdp"),
        P(None, "path", "fsdp"),
        P(),
    )
    out_specs = (
        P(None, "path", "fsdp"),
        P(None, "path", "fsdp"),
        P(None, "path", "fsdp"),
        P(None, "path", "fsdp"),
    )
    return jax.shard_map(body, mesh=mesh, in_specs=in_specs, out_specs=out_specs, check_vma=False)
```

profile of v0, /device:TPU:31, one launch (start us, length us, event | category | flops | bytes accessed | tf_op | source)
XLA Modules:
  0.0 596.4 jit_solution(5396983875467950393)
XLA Ops:
  7.2 0.7 compare_select_fusion
  7.8 0.7 compare_and_fusion
  8.6 4.5 gather_fusion
  13.2 2.8 gather_fusion.1
  15.9 6.3 %broadcast_select_fusion = (bf16[2,8,128,1024]{3,2,1,0:T(8,128)(2,1)}, bf16[2,8,128,1024]{3,2,1,0:T(8,128)(2,1)S(1)}) fusion(bf16[2,8,128,1024]{3,2,1,0:T(8,128)(2,1)} %bitcast.65, pred[2,8]{1,0:T(4,128)(4,1)S(1)} %compare_and_fusion, bf16[2,8,128,1024]{3,2,1,0:T(8,128)(2,1)} %bitcast.64), kind=kLoop, calls=%fused_computation.17 | loop fusion | flops 4194304 | bytes 16777232 | tf_op jit(solution)/shard_map/jit(_take)/select_n | solution.py:90
  22.2 2.6 copy.44
  24.9 5.4 all-to-all-start
  30.3 4.8 copy.45
  35.1 86.9 %all-to-all-done = bf16[2,8,128,1024]{3,2,0,1:T(8,128)(2,1)} async-done(((bf16[2,8,128,1024]{3,2,0,1:T(8,128)(2,1)}), bf16[2,8,128,1024]{3,2,0,1:T(8,128)(2,1)}, u32[]{:S(2)}, u32[]{:S(2)}) %all-to-all-start) | async-done | bytes 4194336 | tf_op jit(solution)/shard_map/all_to_all | solution.py:92
  122.0 5.4 all-to-all-start.1
  127.6 0.8 fusion.24
  128.5 4.2 fusion.42
  132.6 86.4 %all-to-all-done.1 = bf16[2,8,128,1024]{3,2,0,1:T(8,128)(2,1)} async-done(((bf16[2,8,128,1024]{3,2,0,1:T(8,128)(2,1)}), bf16[2,8,128,1024]{3,2,0,1:T(8,128)(2,1)}, u32[]{:S(2)}, u32[]{:S(2)}) %all-to-all-start.1) | async-done | bytes 4194336 | tf_op jit(solution)/shard_map/all_to_all | solution.py:93
  219.1 4.8 fusion.41
  223.9 2.6 fusion.43
  226.6 1.5 convolution_multiply_fusion.4
  228.2 1.3 copy-done.7
  229.6 0.7 all-gather.6.cloned.1.call-update
  230.5 50.5 %all-reduce.3.cloned.1.call-done = f32[512,1024]{1,0:T(8,128)} async-done(((f32[512,1024]{1,0:T(8,128)}), f32[512,1024]{1,0:T(8,128)}) %all-reduce.3.cloned.1.call-update) | async-done | bytes 2097168 | tf_op jit(solution)/shard_map/psum | solution.py:38
  281.0 2.0 multiply_reduce_fusion.1
  283.2 4.2 fusion.40
  287.5 12.3 %all-gather.6.cloned.1.call-done = bf16[1,512,1024]{2,1,0:T(8,128)(2,1)} async-done(((bf16[1,128,1024]{2,1,0:T(8,128)(2,1)}), bf16[1,512,1024]{2,1,0:T(8,128)(2,1)}) %all-gather.6.cloned.1.call-update) | async-done | bytes 1048592 | tf_op jit(solution)/shard_map/all_gather | solution.py:34
  299.7 5.0 fusion.8
  304.8 2.6 convolution_multiply_fusion.3
  307.4 3.4 convolution_multiply_fusion.1
  310.8 47.9 %all-reduce.5.cloned.1.call-done = f32[512,1024]{1,0:T(8,128)} async-done(((f32[512,1024]{1,0:T(8,128)}), f32[512,1024]{1,0:T(8,128)}) %all-reduce.5.cloned.1.call-update) | async-done | bytes 2097168 | tf_op jit(solution)/shard_map/psum | solution.py:38
  358.7 2.1 multiply_reduce_fusion
  360.9 1.5 add_convert_fusion
  362.4 8.1 %convolution_multiply_fusion.2 = f32[1024,1024]{1,0:T(8,128)} fusion(bf16[512,1024]{1,0:T(8,128)(2,1)} %all-gather.4.cloned.1.call-done, f32[512,1024]{1,0:T(8,128)} %copy-done.16, bf16[512,1024]{1,0:T(8,128)(2,1)} %add_convert_fusion, bf16[1024,1024]{1,0:T(8,128)(2,1)} %bitcast.73), kind=kOutput, calls=%fused_computation.23 | convolution fusion | flops 2159542272 | bytes 10485760 | tf_op jit(solution)/shard_map/dot_general | solution.py:50
  370.5 5.4 fusion
  375.9 5.6 all-to-all-start.2
  381.5 3.6 multiply_bitcast_fusion
  385.1 5.5 copy.60
  390.6 1.4 convolution_multiply_fusion
  392.0 0.7 copy-done.4
  392.8 2.6 fusion.1
  395.3 77.8 %all-to-all-done.2 = bf16[2,8,128,1024]{3,2,0,1:T(8,128)(2,1)} async-done(((bf16[2,8,128,1024]{3,2,0,1:T(8,128)(2,1)}), bf16[2,8,128,1024]{3,2,0,1:T(8,128)(2,1)}, u32[]{:S(2)}, u32[]{:S(2)}) %all-to-all-start.2) | async-done | bytes 4194336 | tf_op jit(solution)/shard_map/all_to_all | solution.py:126
  473.1 5.4 all-to-all-start.3
  478.8 2.6 copy.70
  481.4 4.3 copy.61
  485.7 84.4 %all-to-all-done.3 = bf16[2,8,128,1024]{3,2,0,1:T(8,128)(2,1)} async-done(((bf16[2,8,128,1024]{3,2,0,1:T(8,128)(2,1)}), bf16[2,8,128,1024]{3,2,0,1:T(8,128)(2,1)}, u32[]{:S(2)}, u32[]{:S(2)}) %all-to-all-start.3) | async-done | bytes 4194336 | tf_op jit(solution)/shard_map/all_to_all | solution.py:127
  570.1 2.6 copy.69
  572.8 2.3 copy.62
  575.1 0.7 convolution_divide_fusion.1
  575.9 0.7 convolution_divide_fusion
  576.6 0.9 copy-done.2
  578.0 0.6 copy-done.9
  579.3 10.6 %fusion.2 = (bf16[8,128,1024]{2,1,0:T(8,128)(2,1)}, bf16[8,128,1024]{2,1,0:T(8,128)(2,1)}, bf16[8,128,1024]{2,1,0:T(8,128)(2,1)}, bf16[8,128,1024]{2,1,0:T(8,128)(2,1)}) fusion(bf16[8,128,1024]{2,1,0:T(8,128)(2,1)S(1)} %copy-done.9, f32[8,128,1024]{2,0,1:T(8,128)S(1)} %bitcast.72, bf16[8,128,1024]{2,1,0:T(8,128)(2,1)S(1)} %copy-done.2, ...), kind=kLoop, calls=%fused_computation.12 | loop fusion | flops 20971520 | bytes 25165824 | tf_op jit(solution)/shard_map/convert_element_type | solution.py:75
  (51 shorter events, 2.6 us)
Async XLA Ops:
  8.6 4.5 copy-start.1
  24.9 97.1 %all-to-all-start = ((bf16[2,8,128,1024]{3,2,0,1:T(8,128)(2,1)}), bf16[2,8,128,1024]{3,2,0,1:T(8,128)(2,1)}, u32[]{:S(2)}, u32[]{:S(2)}) async-start(bf16[2,8,128,1024]{3,2,0,1:T(8,128)(2,1)} %copy.44), calls=%async_computation | async-start | bytes 8388608 | tf_op jit(solution)/shard_map/all_to_all | solution.py:92
  35.1 92.3 %copy-start.8 = (bf16[1,128,1024]{2,1,0:T(8,128)(2,1)S(1)}, bf16[1,128,1024]{2,1,0:T(8,128)(2,1)}, u32[]{:S(2)}) copy-start(bf16[1,128,1024]{2,1,0:T(8,128)(2,1)} %param.9) | copy-start | bytes 786436
  122.0 97.1 %all-to-all-start.1 = ((bf16[2,8,128,1024]{3,2,0,1:T(8,128)(2,1)}), bf16[2,8,128,1024]{3,2,0,1:T(8,128)(2,1)}, u32[]{:S(2)}, u32[]{:S(2)}) async-start(bf16[2,8,128,1024]{3,2,0,1:T(8,128)(2,1)} %copy.45), calls=%async_computation.1 | async-start | bytes 8388608 | tf_op jit(solution)/shard_map/all_to_all | solution.py:93
  127.4 96.5 %all-gather.4.cloned.1.call-start = ((), (), s32[]{:S(2)}) async-start(), calls=%async_computation.4 | async-start | bytes 1310720 | tf_op jit(solution)/shard_map/all_gather | solution.py:34
  128.4 152.6 %all-reduce.3.cloned.1.call-start = ((), (), s32[]{:S(2)}) async-start(), calls=%async_computation.5 | async-start | bytes 4194304 | tf_op jit(solution)/shard_map/psum | solution.py:38
  223.9 2.6 copy-start.11
  226.5 1.5 copy-start.16
  228.2 1.3 copy-start.7
  229.5 70.2 %all-gather.6.cloned.1.call-start = ((), (), s32[]{:S(2)}) async-start(), calls=%async_computation.7 | async-start | bytes 1310720 | tf_op jit(solution)/shard_map/all_gather | solution.py:34
  230.3 128.4 %all-reduce.5.cloned.1.call-start = ((), (), s32[]{:S(2)}) async-start(), calls=%async_computation.6 | async-start | bytes 4194304 | tf_op jit(solution)/shard_map/psum | solution.py:38
  281.0 2.2 copy-start
  299.7 5.0 copy-start.12
  310.8 50.0 %copy-start.13 = (bf16[1,512,1024]{2,1,0:T(8,128)(2,1)S(1)}, bf16[1,512,1024]{2,1,0:T(8,128)(2,1)}, u32[]{:S(2)}) copy-start(bf16[1,512,1024]{2,1,0:T(8,128)(2,1)} %all-gather.6.cloned.1.call-done) | copy-start | bytes 3145732
  358.7 2.2 copy-start.5
  375.9 5.6 copy-start.18
  375.9 97.2 %all-to-all-start.2 = ((bf16[2,8,128,1024]{3,2,0,1:T(8,128)(2,1)}), bf16[2,8,128,1024]{3,2,0,1:T(8,128)(2,1)}, u32[]{:S(2)}, u32[]{:S(2)}) async-start(bf16[2,8,128,1024]{3,2,0,1:T(8,128)(2,1)} %fusion), calls=%async_computation.2 | async-start | bytes 8388608 | tf_op jit(solution)/shard_map/all_to_all | solution.py:126
  385.1 5.5 copy-start.14
  385.1 5.5 copy-start.17
  390.6 2.2 copy-start.4
  395.3 83.2 %copy-start.15 = (s32[8,2]{0,1:T(2,128)S(1)}, s32[8,2]{0,1:T(2,128)}, u32[]{:S(2)}) copy-start(s32[8,2]{0,1:T(2,128)} %param.15) | copy-start | bytes 196
  473.1 97.0 %all-to-all-start.3 = ((bf16[2,8,128,1024]{3,2,0,1:T(8,128)(2,1)}), bf16[2,8,128,1024]{3,2,0,1:T(8,128)(2,1)}, u32[]{:S(2)}, u32[]{:S(2)}) async-start(bf16[2,8,128,1024]{3,2,0,1:T(8,128)(2,1)} %fusion.1), calls=%async_computation.3 | async-start | bytes 8388608 | tf_op jit(solution)/shard_map/all_to_all | solution.py:127
  572.8 2.3 copy-start.6
  575.8 1.6 copy-start.2
  575.8 2.2 copy-start.3
  575.8 2.8 copy-start.9
  575.9 3.4 copy-start.10
Sparse Core Ops, SparseCore 0:
  130.4 18.3 all-gather.3
  229.6 51.3 all-reduce.2
  282.7 17.0 all-gather.5
  307.5 51.1 all-reduce.4
where the time goes:
time: 601 us; the launch traced here: 596 us
  waiting for transfers between devices  447 us (74%)
  local copies, waits for them, and re-layouts  46.6 us (8%)
  matrix products  33.8 us (6%)
  other arithmetic  32.9 us (5%)
  starting transfers between devices  22.2 us (4%)
  between operations  13.9 us (2%)
    psum x2, waiting for transfers between devices, whole_sum(): return lax.psum(values, 'fsdp')  98.4 us
    all_to_all x1, waiting for transfers between devices, body(): lax.all_to_all(send_up, 'path', split_axis=1, concat_axis=1, tiled=True)  86.9 us
    all_to_all x1, waiting for transfers between devices, body(): lax.all_to_all(send_down, 'path', split_axis=1, concat_axis=1, tiled=True)  86.4 us
    all_to_all x1, waiting for transfers between devices, body(): lax.all_to_all(delta_down, 'path', split_axis=1, concat_axis=1, tiled=True)  84.4 us
    all_to_all x1, waiting for transfers between devices, body(): lax.all_to_all(delta_up, 'path', split_axis=1, concat_axis=1, tiled=True)  77.8 us
    dot_general x4, matrix products, over_rows(): lax.dot_general(left, right, (((0,), (0,)), ((), ())), preferred_element_...  16.5 us
    all_gather x2, waiting for transfers between devices, gather_rows(): return lax.all_gather(values, 'fsdp', axis=0, tiled=True)  12.3 us
  transfers between devices with their start and end apart: 8, of which 7 were waited for; matrix products, arithmetic and copies ran while one was open for 7% of the time, Pallas kernels for 0%

commit v1 on v0

v1 whole, which is shorter than its diff:
```python
import functools
import math

import jax
import jax.numpy as jnp
from jax import lax
from jax.experimental import pallas as pl
from jax.experimental.pallas import tpu as pltpu
from jax.sharding import PartitionSpec as P

inner_rate = 2.0
outer_rate = 0.7
keep_rate = 0.9
norm_eps = 1e-06
tanh_coeff = 0.7978845608028654
cube_coeff = 0.044715
MESH = pl.DeviceIdType.MESH


def gelu_both(values):
    inside = tanh_coeff * (values + cube_coeff * values * values * values)
    tangent = jnp.tanh(inside)
    value = 0.5 * values * (1.0 + tangent)
    slope = 0.5 * (1.0 + tangent) + 0.5 * values * (1.0 - tangent * tangent) * tanh_coeff * (
        1.0 + 3.0 * cube_coeff * values * values
    )
    return value, slope


def row_scale(values):
    return lax.rsqrt(jnp.mean(values * values, axis=-1, keepdims=True) + norm_eps)


def dot(left, right, dims=((1,), (0,))):
    return lax.dot_general(left, right, (dims, ((), ())), preferred_element_type=jnp.float32)


def each(count, act):
    def step(j, carry):
        act(j)
        return carry

    lax.fori_loop(1, count, step, 0)


def tiles(total, size, act):
    def step(j, carry):
        act(pl.ds(pl.multiple_of(j * size, size), size))
        return carry

    lax.fori_loop(0, total // size, step, 0)


def window_kernel(
    paths, shards, x_ref, g_ref, send_up, send_down, came,
    wbuf, gbuf, norm1, norm2, cot, backmid, hid1, hid2, backpre, slope1, slope2,
    part, sums, middle,
    w_send, w_recv, g_send, g_recv, a_send, a_recv, r_send, r_recv, local_w, local_g,
):
    me = lax.axis_index("path")
    mine = lax.axis_index("fsdp")
    piece, cols = send_up.shape[1:]
    rows, depth = x_ref.shape
    in_scale = 1.0 / math.sqrt(depth)
    hid_scale = 1.0 / math.sqrt(cols * shards)
    tile = 256

    def block(at, size):
        return pl.ds(pl.multiple_of(at * size, size), size)

    def weight_copy(k, j, to):
        source = (send_up, send_down)[k % 2]
        return pltpu.make_async_remote_copy(
            src_ref=source.at[(k // 2) * paths + to],
            dst_ref=wbuf.at[k, block(me, piece)],
            send_sem=w_send.at[k, j], recv_sem=w_recv.at[k, j],
            device_id=(to, mine), device_id_type=MESH,
        )

    def weight_start(k):
        each(paths, lambda j: weight_copy(k, j, lax.rem(me + j, paths)).start())

    def weight_own(k):
        source = (send_up, send_down)[k % 2]
        return pltpu.make_async_copy(
            source.at[(k // 2) * paths + me], wbuf.at[k, block(me, piece)], local_w.at[k]
        )

    def weight_wait(k):
        def act(j):
            origin = lax.rem(me + paths - j, paths)
            pltpu.make_async_remote_copy(
                src_ref=wbuf.at[k, block(origin, piece)],
                dst_ref=wbuf.at[k, block(origin, piece)],
                send_sem=w_send.at[k, j], recv_sem=w_recv.at[k, j],
                device_id=(origin, mine), device_id_type=MESH,
            ).wait_recv()

        each(paths, act)
        weight_own(k).wait()

    def grad_copy(k, j, to):
        return pltpu.make_async_remote_copy(
            src_ref=gbuf.at[k, block(to, piece)],
            dst_ref=came.at[k, me],
            send_sem=g_send.at[k, j], recv_sem=g_recv.at[k, j],
            device_id=(to, mine), device_id_type=MESH,
        )

    def grad_own(k):
        return pltpu.make_async_copy(gbuf.at[k, block(me, piece)], came.at[k, me], local_g.at[k])

    def grad_start(k):
        each(paths, lambda j: grad_copy(k, j, lax.rem(me + j, paths)).start())
        grad_own(k).start()

    def grad_wait(k):
        def act(j):
            origin = lax.rem(me + paths - j, paths)
            pltpu.make_async_remote_copy(
                src_ref=came.at[k, origin], dst_ref=came.at[k, origin],
                send_sem=g_send.at[k, j], recv_sem=g_recv.at[k, j],
                device_id=(origin, mine), device_id_type=MESH,
            ).wait_recv()

        each(paths, act)
        grad_own(k).wait()

    def rows_copy(i, buf, at, j, to):
        return pltpu.make_async_remote_copy(
            src_ref=buf.at[block(at, rows)], dst_ref=buf.at[block(at, rows)],
            send_sem=a_send.at[i, j], recv_sem=a_recv.at[i, j],
            device_id=(me, to), device_id_type=MESH,
        )

    def rows_start(i, buf):
        each(shards, lambda j: rows_copy(i, buf, mine, j, lax.rem(mine + j, shards)).start())

    def rows_wait(i, buf):
        def act(j):
            origin = lax.rem(mine + shards - j, shards)
            rows_copy(i, buf, origin, j, origin).wait_recv()

        each(shards, act)

    def sum_copy(i, j, to):
        return pltpu.make_async_remote_copy(
            src_ref=part.at[i, to], dst_ref=sums.at[i, j],
            send_sem=r_send.at[i, j], recv_sem=r_recv.at[i, j],
            device_id=(me, to), device_id_type=MESH,
        )

    def sum_parts(i, left, k, factor):
        def product(to):
            part[i, to] = dot(left[block(to, rows), :], wbuf[k], ((1,), (1,))) * factor

        def act(j):
            to = lax.rem(mine + j, shards)
            product(to)
            sum_copy(i, j, to).start()

        each(shards, act)
        product(mine)

    def sum_wait(i):
        each(shards, lambda j: sum_copy(i, j, lax.rem(mine + j, shards)).wait_recv())
        total = part[i, mine]
        for j in range(1, shards):
            total = total + sums[i, j]
        return total

    def grad_product(k, left, right, factor):
        def act(at):
            gbuf[k, :, at] = (
                inner_rate * (dot(left[...], right[:, at], ((0,), (0,))) * factor)
            ).astype(jnp.bfloat16)

        tiles(cols, tile, act)
        grad_start(k)

    barrier = pltpu.get_barrier_semaphore()
    each(paths, lambda j: pl.semaphore_signal(
        barrier, inc=1, device_id=(lax.rem(me + j, paths), mine), device_id_type=MESH))
    each(shards, lambda j: pl.semaphore_signal(
        barrier, inc=1, device_id=(me, lax.rem(mine + j, shards)), device_id_type=MESH))
    pl.semaphore_wait(barrier, paths + shards - 2)

    weight_start(0)
    weight_start(1)
    for k in range(4):
        weight_own(k).start()
    tokens = x_ref[...].astype(jnp.float32)
    norm1[block(mine, rows), :] = (tokens * row_scale(tokens)).astype(jnp.bfloat16)
    rows_start(0, norm1)
    cot[block(mine, rows), :] = g_ref[...]
    rows_start(1, cot)
    rows_wait(0, norm1)

    weight_wait(0)
    weight_start(2)

    def forward_first(at):
        value, slope = gelu_both(dot(norm1[...], wbuf[0, :, at]) * in_scale)
        hid1[:, at] = value.astype(jnp.bfloat16)
        slope1[:, at] = slope

    tiles(cols, tile, forward_first)

    weight_wait(1)
    weight_start(3)
    sum_parts(0, hid1, 1, hid_scale)
    mid = x_ref[...].astype(jnp.float32) + sum_wait(0)
    middle[...] = mid
    norm2[block(mine, rows), :] = (mid * row_scale(mid)).astype(jnp.bfloat16)
    rows_start(2, norm2)
    rows_wait(2, norm2)
    rows_wait(1, cot)

    weight_wait(2)

    def forward_second(at):
        value, slope = gelu_both(dot(norm2[...], wbuf[2, :, at]) * in_scale)
        hid2[:, at] = value.astype(jnp.bfloat16)
        slope2[:, at] = slope

    tiles(cols, tile, forward_second)
    grad_product(3, cot, hid2, hid_scale)

    weight_wait(3)

    def back_second(at):
        back = dot(cot[...], wbuf[3, :, at]) * hid_scale
        backpre[1, :, at] = (back * slope2[:, at]).astype(jnp.bfloat16)

    tiles(cols, tile, back_second)
    sum_parts(1, backpre.at[1], 2, in_scale)
    grad_product(2, norm2, backpre.at[1], in_scale)

    back_normed = sum_wait(1)
    mid = middle[...]
    scale = row_scale(mid)
    unit = mid * scale
    centred = back_normed - unit * jnp.mean(back_normed * unit, axis=-1, keepdims=True)
    backmid[block(mine, rows), :] = (
        g_ref[...].astype(jnp.float32) + scale * centred
    ).astype(jnp.bfloat16)
    rows_start(3, backmid)
    rows_wait(3, backmid)
    grad_product(1, backmid, hid1, hid_scale)

    def back_first(at):
        back = dot(backmid[...], wbuf[1, :, at]) * hid_scale
        backpre[0, :, at] = (back * slope1[:, at]).astype(jnp.bfloat16)

    tiles(cols, tile, back_first)
    grad_product(0, norm1, backpre.at[0], in_scale)

    for k in (3, 2, 1, 0):
        grad_wait(k)
    for k in range(4):
        each(paths, lambda j: weight_copy(k, j, lax.rem(me + j, paths)).wait_send())
        each(paths, lambda j: grad_copy(k, j, lax.rem(me + j, paths)).wait_send())
    for i, buf in enumerate((norm1, cot, norm2, backmid)):
        each(shards, lambda j: rows_copy(i, buf, mine, j, lax.rem(mine + j, shards)).wait_send())
    for i in range(2):
        each(shards, lambda j: sum_copy(i, j, lax.rem(mine + j, shards)).wait_send())


def window(paths, shards, tokens, cotangent, send_up, send_down):
    piece, cols = send_up.shape[1:]
    rows, depth = tokens.shape
    total = rows * shards
    bf16, f32 = jnp.bfloat16, jnp.float32
    vmem = pl.BlockSpec(memory_space=pltpu.VMEM)
    anywhere = pl.BlockSpec(memory_space=pl.ANY)
    dma = pltpu.SemaphoreType.DMA
    return pl.pallas_call(
        functools.partial(window_kernel, paths, shards),
        out_shape=jax.ShapeDtypeStruct((4, paths, piece, cols), bf16),
        in_specs=[vmem, vmem, anywhere, anywhere],
        out_specs=anywhere,
        scratch_shapes=[
            pltpu.VMEM((4, depth, cols), bf16),
            pltpu.VMEM((4, depth, cols), bf16),
            pltpu.VMEM((total, depth), bf16),
            pltpu.VMEM((total, depth), bf16),
            pltpu.VMEM((total, depth), bf16),
            pltpu.VMEM((total, depth), bf16),
            pltpu.VMEM((total, cols), bf16),
            pltpu.VMEM((total, cols), bf16),
            pltpu.VMEM((2, total, cols), bf16),
            pltpu.VMEM((total, cols), f32),
            pltpu.VMEM((total, cols), f32),
            pltpu.VMEM((2, shards, rows, depth), f32),
            pltpu.VMEM((2, shards, rows, depth), f32),
            pltpu.VMEM((rows, depth), f32),
            dma((4, paths)), dma((4, paths)),
            dma((4, paths)), dma((4, paths)),
            dma((4, shards)), dma((4, shards)),
            dma((2, shards)), dma((2, shards)),
            dma((4,)), dma((4,)),
        ],
        compiler_params=pltpu.CompilerParams(
            collective_id=0, has_side_effects=True, vmem_limit_bytes=56 * 1024 * 1024
        ),
        cost_estimate=pl.CostEstimate(
            flops=20 * total * depth * cols,
            bytes_accessed=16 * depth * cols * 2,
            transcendentals=2 * total * cols,
        ),
        name="window",
    )(tokens, cotangent, send_up, send_down)


def pick_kernel(chosen, up_ref, down_ref, send_up, send_down):
    send_up[...] = up_ref[...]
    send_down[...] = down_ref[...]


def pick(chosen, up_weight, down_weight):
    modules, piece, cols = up_weight.shape
    count = chosen.shape[0]
    taken = pl.BlockSpec((1, piece, cols), lambda i, ids: (ids[i], 0, 0))
    put = pl.BlockSpec((1, piece, cols), lambda i, ids: (i, 0, 0))
    out = jax.ShapeDtypeStruct((count, piece, cols), jnp.bfloat16)
    return pl.pallas_call(
        pick_kernel,
        out_shape=(out, out),
        grid_spec=pltpu.PrefetchScalarGridSpec(
            num_scalar_prefetch=1, grid=(count,), in_specs=[taken, taken], out_specs=[put, put]
        ),
        name="pick",
    )(chosen, up_weight, down_weight)


def update_kernel(
    paths, half, chosen, came, up, down, up_mom, down_mom,
    new_up, new_down, new_up_mom, new_down_mom, total,
):
    module = pl.program_id(0)
    base = (module // half) * paths

    def tally(q, count):
        return count + (chosen[base + q] == module).astype(jnp.int32)

    count = lax.fori_loop(0, paths, tally, jnp.int32(0)).astype(jnp.float32)
    for k, weight, moment, new_weight, new_moment in (
        (0, up, up_mom, new_up, new_up_mom),
        (1, down, down_mom, new_down, new_down_mom),
    ):
        total[...] = jnp.zeros_like(total)

        def add(q, carry):
            @pl.when(chosen[base + q] == module)
            def _():
                total[...] += came[k, q].astype(jnp.float32)

            return carry

        lax.fori_loop(0, paths, add, 0)
        mean = total[...] / count
        fresh = keep_rate * moment[0].astype(jnp.float32) + mean
        step = weight[0].astype(jnp.float32) - outer_rate * (mean + keep_rate * fresh)
        new_weight[0] = step.astype(jnp.bfloat16)
        new_moment[0] = fresh.astype(jnp.bfloat16)


def update(chosen, came, up, down, up_mom, down_mom):
    modules, piece, cols = up.shape
    paths = came.shape[1]
    half = modules // 2
    one = pl.BlockSpec((1, piece, cols), lambda m, ids: (m, 0, 0))
    level = pl.BlockSpec((2, paths, piece, cols), lambda m, ids: (m // half, 0, 0, 0))
    out = jax.ShapeDtypeStruct(up.shape, jnp.bfloat16)
    return pl.pallas_call(
        functools.partial(update_kernel, paths, half),
        out_shape=(out,) * 4,
        grid_spec=pltpu.PrefetchScalarGridSpec(
            num_scalar_prefetch=1, grid=(modules,), in_specs=[level] + [one] * 4,
            out_specs=[one] * 4, scratch_shapes=[pltpu.VMEM((piece, cols), jnp.float32)],
        ),
        compiler_params=pltpu.CompilerParams(vmem_limit_bytes=48 * 1024 * 1024),
        name="update",
    )(chosen, came, up, down, up_mom, down_mom)


def body(paths, shards, hidden_in, cotangent, up_weight, down_weight, up_moment, down_moment, sharing):
    chosen = jnp.transpose(sharing).reshape(-1)
    send_up, send_down = pick(chosen, up_weight, down_weight)
    came = window(paths, shards, hidden_in[0], cotangent[0], send_up, send_down)
    return update(chosen, came, up_weight, down_weight, up_moment, down_moment)


def solution(mesh):
    weights = P(None, "path", "fsdp")
    tokens = P("path", "fsdp", None)
    return jax.shard_map(
        functools.partial(body, mesh.shape["path"], mesh.shape["fsdp"]),
        mesh=mesh,
        in_specs=(tokens, tokens, weights, weights, weights, weights, P()),
        out_specs=(weights,) * 4,
        check_vma=False,
    )
```

time: 601 us -> 402 us (0.67)
  waiting for transfers between devices: 447 us -> 0 us
  Pallas kernels: 0 us -> 398 us
  local copies, waits for them, and re-layouts: 46.6 us -> 1.28 us
  matrix products: 33.8 us -> 0 us
  other arithmetic: 32.9 us -> 0 us
  starting transfers between devices: 22.2 us -> 0 us
  between operations: 13.9 us -> 0.67 us
    pallas_call x0 -> x3, Pallas kernels: none -> 398 us  [the longest x1 373 us: window(): pl.pallas_call(functools.partial(window_kernel, paths, shards), out_shape...]
    all_to_all x4 -> x0, waiting for transfers between devices: 336 us -> none  [the longest x1 86.9 us: body(): lax.all_to_all(send_up, 'path', split_axis=1, concat_axis=1, tiled=True)]
    psum x2 -> x0, waiting for transfers between devices: 98.4 us -> none  [whole_sum(): return lax.psum(values, 'fsdp')]
    dot_general x11 -> x0, matrix products: 33.8 us -> none  [the longest x4 16.5 us: over_rows(): lax.dot_general(left, right, (((0,), (0,)), ((), ())), preferred_element_...]
    all_to_all x4 -> x0, starting transfers between devices: 21.9 us -> none  [the longest x1 5.57 us: body(): lax.all_to_all(delta_up, 'path', split_axis=1, concat_axis=1, tiled=True)]
    convert_element_type x5 -> x0, other arithmetic: 20.8 us -> none  [the longest x1 10.6 us: outer_step(): return (new_weight.astype(jnp.bfloat16), new_moment.astype(jnp.bfloat16))]
    all_gather x2 -> x0, waiting for transfers between devices: 12.3 us -> none  [gather_rows(): return lax.all_gather(values, 'fsdp', axis=0, tiled=True)]
    unnamed x40 -> x6, local copies, waits for them, and re-layouts: 11.9 us -> 0.01 us
  transfers between devices with their start and end apart: 8 -> 0, of which waited for: 7 -> 0; matrix products, arithmetic and copies ran while one was open for 7% -> 0% of each run, Pallas kernels for 0% -> 0%
where the time goes in v1:
time: 402 us; the launch traced here: 400 us
  Pallas kernels  398 us (99%)
    pallas_call x1, Pallas kernels, window(): pl.pallas_call(functools.partial(window_kernel, paths, shards), out_shape...  373 us
    pallas_call x1, Pallas kernels, update(): pl.pallas_call(functools.partial(update_kernel, paths, half), out_shape=(...  13.2 us
    pallas_call x1, Pallas kernels, pick(): pl.pallas_call(pick_kernel, out_shape=(out, out), grid_spec=pltpu.Prefetc...  11.8 us

profile of v1, /device:TPU:31, one launch (start us, length us, event | category | flops | bytes accessed | tf_op | source)
XLA Modules:
  0.0 400.2 jit_solution(10961490183030731282)
XLA Ops:
  0.6 1.3 reshape.11.chosen
  1.9 11.8 %pick.1 = (bf16[16,128,1024]{2,1,0:T(8,128)(2,1)}, bf16[16,128,1024]{2,1,0:T(8,128)(2,1)}) custom-call(s32[16]{0:T(128)} %reshape.11.chosen, bf16[8,128,1024]{2,1,0:T(8,128)(2,1)} %up.1, bf16[8,128,1024]{2,1,0:T(8,128)(2,1)} %down.1), custom_call_target="tpu_custom_call" | custom-call | tf_op jit(solution)/shard_map/pick/pallas_call | solution.py:326
  13.7 0.0 copy-start
  13.7 0.0 copy-start.1
  13.7 0.0 copy-start.2
  13.7 373.2 %window.1.came = bf16[4,8,128,1024]{3,2,1,0:T(8,128)(2,1)} custom-call(bf16[128,1024]{1,0:T(8,128)(2,1)} %bitcast.3, bf16[128,1024]{1,0:T(8,128)(2,1)} %bitcast.4, bf16[16,128,1024]{2,1,0:T(8,128)(2,1)} %get-tuple-element.6.send_up, bf16[16,128,1024]{2,1,0:T(8,128)(2,1)} %get-tuple-element.7.send_down), custom_call_target="tpu_custom_call" | custom-call | flops 10737418240 | bytes 33554432 | tf_op jit(solution)/shard_map/window/pallas_call | solution.py:277
  387.0 0.0 copy-done
  387.0 0.0 copy-done.1
  387.0 0.0 copy-done.2
  387.0 13.2 %update.1 = (bf16[8,128,1024]{2,1,0:T(8,128)(2,1)}, bf16[8,128,1024]{2,1,0:T(8,128)(2,1)}, bf16[8,128,1024]{2,1,0:T(8,128)(2,1)}, bf16[8,128,1024]{2,1,0:T(8,128)(2,1)}) custom-call(s32[16]{0:T(128)S(1)} %copy-done.2, bf16[4,8,128,1024]{3,2,1,0:T(8,128)(2,1)} %window.1.came, bf16[8,128,1024]{2,1,0:T(8,128)(2,1)S(1)} %copy-done, ...), custom_call_target="tpu_custom_call" | custom-call | tf_op jit(solution)/shard_map/update/pallas_call | solution.py:375
Async XLA Ops:
  13.7 373.2 %copy-start = (bf16[8,128,1024]{2,1,0:T(8,128)(2,1)S(1)}, bf16[8,128,1024]{2,1,0:T(8,128)(2,1)}, u32[]{:S(2)}) copy-start(bf16[8,128,1024]{2,1,0:T(8,128)(2,1)} %up.1) | copy-start | bytes 6291460
  13.7 373.3 %copy-start.1 = (bf16[8,128,1024]{2,1,0:T(8,128)(2,1)S(1)}, bf16[8,128,1024]{2,1,0:T(8,128)(2,1)}, u32[]{:S(2)}) copy-start(bf16[8,128,1024]{2,1,0:T(8,128)(2,1)} %down.1) | copy-start | bytes 6291460
  13.7 373.3 %copy-start.2 = (s32[16]{0:T(128)S(1)}, s32[16]{0:T(128)}, u32[]{:S(2)}) copy-start(s32[16]{0:T(128)} %reshape.11.chosen) | copy-start | bytes 196

commit v2 on v0

v2 whole, which is shorter than its diff:
```python
import functools
import math

import jax
import jax.numpy as jnp
from jax import lax
from jax.experimental import pallas as pl
from jax.experimental.pallas import tpu as pltpu
from jax.sharding import PartitionSpec as P

inner_rate = 2.0
outer_rate = 0.7
keep_rate = 0.9
norm_eps = 1e-06
tanh_coeff = 0.7978845608028654
cube_coeff = 0.044715
MESH = pl.DeviceIdType.MESH


def gelu_both(values):
    inside = tanh_coeff * (values + cube_coeff * values * values * values)
    tangent = jnp.tanh(inside)
    value = 0.5 * values * (1.0 + tangent)
    slope = 0.5 * (1.0 + tangent) + 0.5 * values * (1.0 - tangent * tangent) * tanh_coeff * (
        1.0 + 3.0 * cube_coeff * values * values
    )
    return value, slope


def row_scale(values):
    return lax.rsqrt(jnp.mean(values * values, axis=-1, keepdims=True) + norm_eps)


def dot(left, right, dims=((1,), (0,))):
    return lax.dot_general(left, right, (dims, ((), ())), preferred_element_type=jnp.float32)


def loop(first, count, act):
    def step(j, carry):
        act(j)
        return carry

    lax.fori_loop(first, count, step, 0)


def flipped(value, mask):
    bit = 1
    while bit <= mask:
        if mask & bit:
            value = value + bit * (1 - 2 * lax.rem(lax.div(value, bit), 2))
        bit *= 2
    return value


def masks_above(bit, planes):
    return [m for m in range(planes) if m % (2 * bit) == 0]


def window_kernel(
    planes, across, shards, aligned,
    ids, coefs, x_ref, g_ref, up_ref, down_ref, came_up, came_down,
    relay0, relay1, relay2, relay3, stage, weights, back, norm1, norm2, cot, backmid, hid1, hid2, backpre,
    slope1, slope2, part, outgoing, incoming, own_x, middle,
    z_send, z_recv, p_send, p_recv, g_send, g_recv, m_send, m_recv,
    a_send, a_recv, r_send, r_recv, t_send, t_recv, local_z, local_m,
):
    relay = (relay0, relay1, relay2, relay3)
    path = lax.axis_index("path")
    shard = lax.axis_index("fsdp")
    plane = lax.div(path, across)
    column = lax.rem(path, across)
    slots = across * shards
    slot = column * shards + shard
    rows, depth = x_ref.shape
    half, piece, narrow = relay0.shape[1:]
    width = narrow * shards * planes
    in_scale = 1.0 / math.sqrt(depth)
    hid_scale = 1.0 / math.sqrt(width)
    bf16, f32 = jnp.bfloat16, jnp.float32
    bits = [1 << b for b in range(planes.bit_length() - 1)]

    def block(at):
        return pl.ds(pl.multiple_of(at * rows, rows), rows)

    def in_plane(to):
        return (plane * across + lax.div(to, shards), lax.rem(to, shards))

    def along(to):
        return (to * across + column, shard)

    def quarter(ref, level, at):
        if aligned:
            return ref.at[
                pl.ds(level * half, half), :, pl.ds(pl.multiple_of(at * narrow, narrow), narrow)
            ]
        return ref.at[at, pl.ds(level * half, half)]

    def remote(src, dst, send, recv, to):
        return pltpu.make_async_remote_copy(
            src_ref=src, dst_ref=dst, send_sem=send, recv_sem=recv,
            device_id=to, device_id_type=MESH,
        )

    def z_copy(k, j, to):
        source = (up_ref, down_ref)[k % 2]
        return remote(quarter(source, k // 2, to), relay[k].at[plane],
                      z_send.at[k, j], z_recv.at[k, j], along(to))

    def z_own(k):
        source = (up_ref, down_ref)[k % 2]
        return pltpu.make_async_copy(
            quarter(source, k // 2, plane), relay[k].at[plane], local_z.at[k])

    def z_start(k):
        loop(1, planes, lambda j: z_copy(k, j, lax.rem(plane + j, planes)).start())

    def z_wait(k):
        def act(j):
            origin = lax.rem(plane + planes - j, planes)
            remote(relay[k].at[origin], relay[k].at[origin],
                   z_send.at[k, j], z_recv.at[k, j], along(origin)).wait_recv()

        loop(1, planes, act)
        z_own(k).wait()

    def p_copy(k, j, to):
        return remote(stage.at[k, to], weights.at[k, shard, :, column],
                      p_send.at[k, j], p_recv.at[k, j], in_plane(to))

    def p_start(k):
        def act(j):
            to = lax.rem(slot + j, slots)
            stage[k, to] = relay[k][:, ids[(k // 2) * slots + to]]
            p_copy(k, j, to).start()

        loop(1, slots, act)
        weights[k, shard, :, column] = relay[k][:, ids[(k // 2) * slots + slot]]

    def p_wait(k):
        def act(j):
            origin = lax.rem(slot + slots - j, slots)
            land = weights.at[k, lax.rem(origin, shards), :, lax.div(origin, shards)]
            remote(land, land, p_send.at[k, j], p_recv.at[k, j], in_plane(origin)).wait_recv()

        loop(1, slots, act)

    def p_sent(k):
        loop(1, slots, lambda j: p_copy(k, j, lax.rem(slot + j, slots)).wait_send())

    def weight(k, at):
        return weights[k, at].reshape(depth, narrow)

    def g_copy(k, j, to):
        return remote(stage.at[k, to], back.at[k, slot],
                      g_send.at[k, j], g_recv.at[k, j], in_plane(to))

    def g_start(k, left, right, factor):
        p_sent(k)

        def act(at):
            value = inner_rate * (dot(left[...], right[at], ((0,), (0,))) * factor)
            value = value.astype(bf16).reshape(planes, across, piece, narrow)
            for c in range(across):
                stage[k, c * shards + at] = value[:, c]

        loop(0, shards, act)
        loop(1, slots, lambda j: g_copy(k, j, lax.rem(slot + j, slots)).start())
        back[k, slot] = stage[k, slot]

    def g_wait(k):
        def act(j):
            origin = lax.rem(slot + slots - j, slots)
            remote(back.at[k, origin], back.at[k, origin],
                   g_send.at[k, j], g_recv.at[k, j], in_plane(origin)).wait_recv()

        loop(1, slots, act)

    def m_copy(k, j, to):
        target = (came_up, came_down)[k % 2]
        return remote(relay[k].at[to], quarter(target, k // 2, plane),
                      m_send.at[k, j], m_recv.at[k, j], along(to))

    def m_own(k):
        target = (came_up, came_down)[k % 2]
        return pltpu.make_async_copy(
            relay[k].at[plane], quarter(target, k // 2, plane), local_m.at[k])

    def m_start(k):
        g_wait(k)
        strip = 32
        strips = piece // strip
        batch = min(4, half)

        def act(at):
            to = lax.div(at, strips)
            lines = pl.ds(pl.multiple_of(lax.rem(at, strips) * strip, strip), strip)
            for first in range(0, half, batch):
                totals = [jnp.zeros((strip, narrow), f32)] * batch
                for t in range(slots):
                    value = back[k, t, to, lines, :].astype(f32)
                    totals = [
                        total + coefs[((k // 2) * half + first + m) * slots + t] * value
                        for m, total in enumerate(totals)
                    ]
                for m, total in enumerate(totals):
                    relay[k][to, first + m, lines, :] = total.astype(bf16)

        loop(0, planes * strips, act)
        loop(1, planes, lambda j: m_copy(k, j, lax.rem(plane + j, planes)).start())
        m_own(k).start()

    def m_wait(k):
        target = (came_up, came_down)[k % 2]

        def act(j):
            origin = lax.rem(plane + planes - j, planes)
            land = quarter(target, k // 2, origin)
            remote(land, land, m_send.at[k, j], m_recv.at[k, j], along(origin)).wait_recv()

        loop(1, planes, act)
        m_own(k).wait()

    gather_plan = []
    for bit in reversed(bits):
        for mask in masks_above(bit, planes):
            gather_plan.append((bit, mask))

    def a_copy(i, buf, c):
        bit, mask = gather_plan[c]
        at = block(flipped(plane, mask))
        return remote(buf.at[at], buf.at[at], a_send.at[i, c], a_recv.at[i, c],
                      along(flipped(plane, bit)))

    def a_start(i, buf, bit):
        for c, step in enumerate(gather_plan):
            if step[0] == bit:
                a_copy(i, buf, c).start()

    def a_wait(i, buf, bit):
        for c, step in enumerate(gather_plan):
            if step[0] == bit:
                at = block(flipped(flipped(plane, bit), step[1]))
                remote(buf.at[at], buf.at[at], a_send.at[i, c], a_recv.at[i, c],
                       along(flipped(plane, bit))).wait_recv()

    def a_through(i, buf):
        for bit in reversed(bits[1:]):
            a_start(i, buf, bit)
            a_wait(i, buf, bit)
        a_start(i, buf, 1)

    sum_plan = []
    for bit in bits:
        for mask in masks_above(bit, planes):
            sum_plan.append((bit, mask))

    def r_copy(i, c):
        return remote(outgoing.at[c], incoming.at[i % incoming.shape[0], c], r_send.at[i, c], r_recv.at[i, c],
                      along(flipped(plane, sum_plan[c][0])))

    def products(left, k, factor):
        def act(at):
            total = dot(left[0, block(at), :], weight(k, 0), ((1,), (1,)))
            for c in range(1, shards):
                total = total + dot(left[c, block(at), :], weight(k, c), ((1,), (1,)))
            part[at] = total * factor

        loop(0, planes, act)

    def r_start(i, bit):
        for c, (of, mask) in enumerate(sum_plan):
            if of == bit:
                outgoing[c] = part[flipped(flipped(plane, bit), mask)].astype(bf16)
                r_copy(i, c).start()

    def r_wait(i, bit):
        for c, (of, mask) in enumerate(sum_plan):
            if of == bit:
                r_copy(i, c).wait_recv()
                at = flipped(plane, mask)
                part[at] = part[at] + incoming[i % incoming.shape[0], c].astype(f32)

    def r_through(i):
        for bit in bits[1:]:
            r_start(i, bit)
            r_wait(i, bit)
        return part[plane]

    token_to = (shard * across + lax.div(path, shards), lax.rem(path, shards))
    token_from = (slot, plane)
    away = jnp.logical_or(token_to[0] != path, token_to[1] != shard)

    def t_copy(i, to, at):
        land = (own_x, cot.at[block(at)])[i]
        return remote((x_ref, g_ref)[i], land, t_send.at[i], t_recv.at[i], to)

    def greet(to):
        pl.semaphore_signal(barrier, inc=1, device_id=to, device_id_type=MESH)

    barrier = pltpu.get_barrier_semaphore()
    loop(1, planes, lambda j: greet(along(lax.rem(plane + j, planes))))
    loop(1, slots, lambda j: greet(in_plane(lax.rem(slot + j, slots))))

    @pl.when(away)
    def _():
        greet(token_to)
        greet(token_from)
        pl.semaphore_wait(barrier, planes + slots)
        t_copy(0, token_to, shard).start()

    @pl.when(jnp.logical_not(away))
    def _():
        pl.semaphore_wait(barrier, planes + slots - 2)

    z_start(0)

    @pl.when(away)
    def _():
        t_copy(1, token_to, shard).start()

    for k in range(4):
        z_own(k).start()

    @pl.when(away)
    def _():
        t_copy(0, token_from, plane).wait_recv()

    @pl.when(jnp.logical_not(away))
    def _():
        own_x[...] = x_ref[...]
        cot[block(plane), :] = g_ref[...]

    tokens = own_x[...].astype(f32)
    norm1[block(plane), :] = (tokens * row_scale(tokens)).astype(bf16)
    a_start(0, norm1, bits[-1])
    z_start(1)
    a_wait(0, norm1, bits[-1])
    for bit in reversed(bits[:-1]):
        a_start(0, norm1, bit)
        if bit > 1:
            a_wait(0, norm1, bit)

    @pl.when(away)
    def _():
        t_copy(1, token_from, plane).wait_recv()

    z_wait(0)
    z_start(2)
    p_start(0)
    a_start(1, cot, bits[-1])
    z_wait(1)
    z_start(3)
    p_start(1)
    a_wait(1, cot, bits[-1])
    for bit in reversed(bits[:-1]):
        a_start(1, cot, bit)
        if bit > 1:
            a_wait(1, cot, bit)
    a_wait(0, norm1, 1)
    p_wait(0)

    def forward_first(at):
        value, slope = gelu_both(dot(norm1[...], weight(0, at)) * in_scale)
        hid1[at] = value.astype(bf16)
        slope1[at] = slope

    loop(0, shards, forward_first)
    z_wait(2)
    p_start(2)
    p_wait(1)
    products(hid1, 1, hid_scale)
    r_start(0, 1)
    r_wait(0, 1)
    mid = own_x[...].astype(f32) + r_through(0)
    middle[...] = mid
    norm2[block(plane), :] = (mid * row_scale(mid)).astype(bf16)
    a_through(2, norm2)
    z_wait(3)
    p_start(3)
    a_wait(2, norm2, 1)
    p_wait(2)

    def forward_second(at):
        value, slope = gelu_both(dot(norm2[...], weight(2, at)) * in_scale)
        hid2[at] = value.astype(bf16)
        slope2[at] = slope

    loop(0, shards, forward_second)
    a_wait(1, cot, 1)
    p_wait(3)

    def back_second(at):
        value = dot(cot[...], weight(3, at)) * hid_scale
        backpre[at] = (value * slope2[at]).astype(bf16)

    loop(0, shards, back_second)
    products(backpre, 2, in_scale)
    for c in range(planes - 1):
        r_copy(0, c).wait_send()
    r_start(1, 1)
    g_start(3, cot, hid2, hid_scale)
    r_wait(1, 1)
    if len(bits) > 1:
        r_start(1, bits[1])
    g_start(2, norm2, backpre, in_scale)
    for bit in bits[1:]:
        r_wait(1, bit)
        if bit != bits[-1]:
            r_start(1, 2 * bit)
    back_normed = part[plane]
    mid = middle[...]
    scale = row_scale(mid)
    unit = mid * scale
    centred = back_normed - unit * jnp.mean(back_normed * unit, axis=-1, keepdims=True)
    backmid[block(plane), :] = (cot[block(plane), :].astype(f32) + scale * centred).astype(bf16)
    a_through(3, backmid)
    a_wait(3, backmid, 1)
    g_start(1, backmid, hid1, hid_scale)

    def back_first(at):
        value = dot(backmid[...], weight(1, at)) * hid_scale
        backpre[at] = (value * slope1[at]).astype(bf16)

    loop(0, shards, back_first)
    g_start(0, norm1, backpre, in_scale)
    for k in (3, 2, 1, 0):
        if k > 1:
            loop(1, planes, lambda j: z_copy(k, j, lax.rem(plane + j, planes)).wait_send())
        m_start(k)
    for k in (3, 2, 1, 0):
        m_wait(k)

    for k in range(4):
        if k < 2:
            loop(1, planes, lambda j: z_copy(k, j, lax.rem(plane + j, planes)).wait_send())
        loop(1, planes, lambda j: m_copy(k, j, lax.rem(plane + j, planes)).wait_send())
        loop(1, slots, lambda j: g_copy(k, j, lax.rem(slot + j, slots)).wait_send())
    for i, buf in enumerate((norm1, cot, norm2, backmid)):
        for c in range(planes - 1):
            a_copy(i, buf, c).wait_send()
    for c in range(planes - 1):
        r_copy(1, c).wait_send()

    @pl.when(away)
    def _():
        t_copy(0, token_to, shard).wait_send()
        t_copy(1, token_to, shard).wait_send()


def window(planes, across, shards, aligned, ids, coefs, tokens, cotangent, up, down):
    half = coefs.shape[0] // (2 * across * shards)
    slots = across * shards
    piece = up.shape[-2]
    narrow = up.shape[-1] // planes if aligned else up.shape[-1]
    rows, depth = tokens.shape
    total = rows * shards
    bf16, f32 = jnp.bfloat16, jnp.float32
    vmem = pl.BlockSpec(memory_space=pltpu.VMEM)
    smem = pl.BlockSpec(memory_space=pltpu.SMEM)
    anywhere = pl.BlockSpec(memory_space=pl.ANY)
    dma = pltpu.SemaphoreType.DMA
    out = jax.ShapeDtypeStruct(up.shape, bf16)
    return pl.pallas_call(
        functools.partial(window_kernel, planes, across, shards, aligned),
        out_shape=(out, out),
        in_specs=[smem, smem, vmem, vmem, anywhere, anywhere],
        out_specs=(anywhere, anywhere),
        scratch_shapes=[
            *[pltpu.VMEM((planes, half, piece, narrow), bf16)] * 4,
            pltpu.VMEM((4, slots, planes, piece, narrow), bf16),
            pltpu.VMEM((4, shards, planes, across, piece, narrow), bf16),
            pltpu.VMEM((4, slots, planes, piece, narrow), bf16),
            pltpu.VMEM((total, depth), bf16),
            pltpu.VMEM((total, depth), bf16),
            pltpu.VMEM((total, depth), bf16),
            pltpu.VMEM((total, depth), bf16),
            pltpu.VMEM((shards, total, narrow), bf16),
            pltpu.VMEM((shards, total, narrow), bf16),
            pltpu.VMEM((shards, total, narrow), bf16),
            pltpu.VMEM((shards, total, narrow), f32),
            pltpu.VMEM((shards, total, narrow), f32),
            pltpu.VMEM((planes, rows, depth), f32),
            pltpu.VMEM((planes - 1, rows, depth), bf16),
            pltpu.VMEM((1 + aligned, planes - 1, rows, depth), bf16),
            pltpu.VMEM((rows, depth), bf16),
            pltpu.VMEM((rows, depth), f32),
            dma((4, planes)), dma((4, planes)),
            dma((4, slots)), dma((4, slots)),
            dma((4, slots)), dma((4, slots)),
            dma((4, planes)), dma((4, planes)),
            dma((4, planes)), dma((4, planes)),
            dma((2, planes)), dma((2, planes)),
            dma((2,)), dma((2,)),
            dma((4,)), dma((4,)),
        ],
        compiler_params=pltpu.CompilerParams(
            collective_id=0, has_side_effects=True, vmem_limit_bytes=61 * 1024 * 1024
        ),
        cost_estimate=pl.CostEstimate(
            flops=20 * total * depth * narrow * shards,
            bytes_accessed=16 * depth * narrow * shards,
            transcendentals=2 * total * narrow * shards,
        ),
        name="window",
    )(ids, coefs, tokens, cotangent, up, down)


def outer_step(weight, moment, mean):
    mean = mean.astype(jnp.float32)
    fresh = keep_rate * moment.astype(jnp.float32) + mean
    step = weight.astype(jnp.float32) - outer_rate * (mean + keep_rate * fresh)
    return step.astype(jnp.bfloat16), fresh.astype(jnp.bfloat16)


def body(paths, shards, hidden_in, cotangent, up_weight, down_weight, up_moment, down_moment, sharing):
    modules, piece, cols = up_weight.shape
    planes = shards
    across = paths // planes
    narrow = cols // planes
    aligned = narrow % 128 == 0
    half = modules // 2
    owners = jnp.transpose(sharing)
    ids = (owners - jnp.array([[0], [half]], jnp.int32)).reshape(-1)
    level = jnp.repeat(owners, half, axis=0)
    member = (level == jnp.arange(modules, dtype=jnp.int32)[:, None]).astype(jnp.float32)
    coefs = (member / jnp.sum(member, axis=1, keepdims=True)).reshape(-1)
    up, down = up_weight, down_weight
    if not aligned:
        up, down = (
            jnp.transpose(v.reshape(modules, piece, planes, narrow), (2, 0, 1, 3))
            for v in (up, down)
        )
    mean_up, mean_down = window(
        planes, across, shards, aligned, ids, coefs, hidden_in[0], cotangent[0], up, down
    )
    if not aligned:
        mean_up, mean_down = (
            jnp.transpose(v, (1, 2, 0, 3)).reshape(modules, piece, cols)
            for v in (mean_up, mean_down)
        )
    new_up, new_up_moment = outer_step(up_weight, up_moment, mean_up)
    new_down, new_down_moment = outer_step(down_weight, down_moment, mean_down)
    return (new_up, new_down, new_up_moment, new_down_moment)


def solution(mesh):
    weights = P(None, "path", "fsdp")
    tokens = P("path", "fsdp", None)
    return jax.shard_map(
        functools.partial(body, mesh.shape["path"], mesh.shape["fsdp"]),
        mesh=mesh,
        in_specs=(tokens, tokens, weights, weights, weights, weights, P()),
        out_specs=(weights,) * 4,
        check_vma=False,
    )
```

time: 601 us -> 371 us (0.62)
  waiting for transfers between devices: 447 us -> 0 us
  Pallas kernels: 0 us -> 358 us
  local copies, waits for them, and re-layouts: 46.6 us -> 1.69 us
  matrix products: 33.8 us -> 0 us
  other arithmetic: 32.9 us -> 9.69 us
  starting transfers between devices: 22.2 us -> 0 us
  between operations: 13.9 us -> 0.66 us
    pallas_call x0 -> x1, Pallas kernels: none -> 358 us  [window(): pl.pallas_call(functools.partial(window_kernel, planes, across, shards, a...]
    all_to_all x4 -> x0, waiting for transfers between devices: 336 us -> none  [the longest x1 86.9 us: body(): lax.all_to_all(send_up, 'path', split_axis=1, concat_axis=1, tiled=True)]
    psum x2 -> x0, waiting for transfers between devices: 98.4 us -> none  [whole_sum(): return lax.psum(values, 'fsdp')]
    dot_general x11 -> x0, matrix products: 33.8 us -> none  [the longest x4 16.5 us: over_rows(): lax.dot_general(left, right, (((0,), (0,)), ((), ())), preferred_element_...]
    all_to_all x4 -> x0, starting transfers between devices: 21.9 us -> none  [the longest x1 5.57 us: body(): lax.all_to_all(delta_up, 'path', split_axis=1, concat_axis=1, tiled=True)]
    convert_element_type x5 -> x1, other arithmetic: 20.8 us -> 7.57 us  [outer_step(): return (step.astype(jnp.bfloat16), fresh.astype(jnp.bfloat16))]
    all_gather x2 -> x0, waiting for transfers between devices: 12.3 us -> none  [gather_rows(): return lax.all_gather(values, 'fsdp', axis=0, tiled=True)]
    unnamed x40 -> x2, local copies, waits for them, and re-layouts: 11.9 us -> 0.01 us
  transfers between devices with their start and end apart: 8 -> 0, of which waited for: 7 -> 0; matrix products, arithmetic and copies ran while one was open for 7% -> 0% of each run, Pallas kernels for 0% -> 0%
where the time goes in v2:
time: 371 us; the launch traced here: 370 us
  Pallas kernels  358 us (96%)
  other arithmetic  9.69 us (3%)
    pallas_call x1, Pallas kernels, window(): pl.pallas_call(functools.partial(window_kernel, planes, across, shards, a...  358 us
    convert_element_type x1, other arithmetic, outer_step(): return (step.astype(jnp.bfloat16), fresh.astype(jnp.bfloat16))  7.57 us

profile of v2, /device:TPU:31, one launch (start us, length us, event | category | flops | bytes accessed | tf_op | source)
XLA Modules:
  0.0 370.4 jit_solution(16009419699894516211)
XLA Ops:
  0.6 0.8 broadcast_subtract_fusion
  1.4 0.6 reshape.30.ids
  2.0 0.8 convert_reduce_fusion
  2.8 0.1 div.13
  2.9 0.1 div.14
  3.0 0.1 div.15
  3.1 0.7 broadcast_in_dim.2
  3.7 0.1 reshape.31
  3.8 0.1 eq.23
  3.9 0.5 fusion.8.coefs
  4.4 0.0 copy-start
  4.4 358.4 %window.1 = (bf16[8,128,1024]{2,1,0:T(8,128)(2,1)}, bf16[8,128,1024]{2,1,0:T(8,128)(2,1)}) custom-call(s32[16]{0:T(128)} %reshape.30.ids, f32[64]{0:T(128)} %fusion.8.coefs, bf16[128,1024]{1,0:T(8,128)(2,1)} %bitcast.6, bf16[128,1024]{1,0:T(8,128)(2,1)} %bitcast.7, bf16[8,128,1024]{2,1,0:T(8,128)(2,1)} %up_ref.1, bf16[8,128,1024]{2,1,0:T(8,128)(2,1)} %down_ref.1), custom_call_target="tpu_custom_call" | custom-call | flops 10737418240 | bytes 16777216 | tf_op jit(solution)/shard_map/window/pallas_call | solution.py:463
  362.8 0.0 copy-done
  362.9 7.6 %fusion.6 = (bf16[8,128,1024]{2,1,0:T(8,128)(2,1)}, bf16[8,128,1024]{2,1,0:T(8,128)(2,1)}, bf16[8,128,1024]{2,1,0:T(8,128)(2,1)}, bf16[8,128,1024]{2,1,0:T(8,128)(2,1)}) fusion(bf16[8,128,1024]{2,1,0:T(8,128)(2,1)} %get-tuple-element.7, bf16[8,128,1024]{2,1,0:T(8,128)(2,1)} %param.13, bf16[8,128,1024]{2,1,0:T(8,128)(2,1)} %down_ref.1, ...), kind=kLoop, calls=%fused_computation.10 | loop fusion | flops 23068672 | bytes 20971520 | tf_op jit(solution)/shard_map/convert_element_type | solution.py:512
  (3 shorter events, 0.0 us)
Async XLA Ops:
  4.4 358.4 %copy-start = (bf16[8,128,1024]{2,1,0:T(8,128)(2,1)S(1)}, bf16[8,128,1024]{2,1,0:T(8,128)(2,1)}, u32[]{:S(2)}) copy-start(bf16[8,128,1024]{2,1,0:T(8,128)(2,1)} %up_ref.1) | copy-start | bytes 6291460

commit v3 on v2

--- a/solution.py
+++ b/solution.py
@@ -333,7 +333,6 @@
     tokens = own_x[...].astype(f32)
     norm1[block(plane), :] = (tokens * row_scale(tokens)).astype(bf16)
     a_start(0, norm1, bits[-1])
-    z_start(1)
     a_wait(0, norm1, bits[-1])
     for bit in reversed(bits[:-1]):
         a_start(0, norm1, bit)
@@ -345,11 +344,11 @@
         t_copy(1, token_from, plane).wait_recv()
 
     z_wait(0)
-    z_start(2)
+    z_start(1)
     p_start(0)
     a_start(1, cot, bits[-1])
     z_wait(1)
-    z_start(3)
+    z_start(2)
     p_start(1)
     a_wait(1, cot, bits[-1])
     for bit in reversed(bits[:-1]):
@@ -365,11 +364,12 @@
         slope1[at] = slope
 
     loop(0, shards, forward_first)
-    z_wait(2)
-    p_start(2)
     p_wait(1)
     products(hid1, 1, hid_scale)
     r_start(0, 1)
+    z_wait(2)
+    z_start(3)
+    p_start(2)
     r_wait(0, 1)
     mid = own_x[...].astype(f32) + r_through(0)
     middle[...] = mid
@@ -414,6 +414,8 @@
     centred = back_normed - unit * jnp.mean(back_normed * unit, axis=-1, keepdims=True)
     backmid[block(plane), :] = (cot[block(plane), :].astype(f32) + scale * centred).astype(bf16)
     a_through(3, backmid)
+    loop(1, planes, lambda j: z_copy(3, j, lax.rem(plane + j, planes)).wait_send())
+    m_start(3)
     a_wait(3, backmid, 1)
     g_start(1, backmid, hid1, hid_scale)
 
@@ -423,15 +425,13 @@
 
     loop(0, shards, back_first)
     g_start(0, norm1, backpre, in_scale)
-    for k in (3, 2, 1, 0):
-        if k > 1:
-            loop(1, planes, lambda j: z_copy(k, j, lax.rem(plane + j, planes)).wait_send())
+    for k in (2, 1, 0):
         m_start(k)
     for k in (3, 2, 1, 0):
         m_wait(k)
 
     for k in range(4):
-        if k < 2:
+        if k < 3:
             loop(1, planes, lambda j: z_copy(k, j, lax.rem(plane + j, planes)).wait_send())
         loop(1, planes, lambda j: m_copy(k, j, lax.rem(plane + j, planes)).wait_send())
         loop(1, slots, lambda j: g_copy(k, j, lax.rem(slot + j, slots)).wait_send())

time: 371 us -> 362 us (0.976)
  Pallas kernels: 358 us -> 349 us
    pallas_call x1, Pallas kernels: 358 us -> 349 us  [window(): pl.pallas_call(functools.partial(window_kernel, planes, across, shards, a...]
where the time goes in v3:
time: 362 us; the launch traced here: 361 us
  Pallas kernels  349 us (96%)
  other arithmetic  9.69 us (3%)
    pallas_call x1, Pallas kernels, window(): pl.pallas_call(functools.partial(window_kernel, planes, across, shards, a...  349 us
    convert_element_type x1, other arithmetic, outer_step(): return (step.astype(jnp.bfloat16), fresh.astype(jnp.bfloat16))  7.57 us

profile of v3, /device:TPU:31, one launch (start us, length us, event | category | flops | bytes accessed | tf_op | source)
XLA Modules:
  0.0 361.4 jit_solution(4197552989009704347)
XLA Ops:
  0.6 0.8 broadcast_subtract_fusion
  1.4 0.6 reshape.30.ids
  2.0 0.8 convert_reduce_fusion
  2.8 0.1 div.13
  2.9 0.1 div.14
  3.0 0.1 div.15
  3.1 0.7 broadcast_in_dim.2
  3.7 0.1 reshape.31
  3.8 0.1 eq.23
  3.9 0.5 fusion.8.coefs
  4.4 0.0 copy-start
  4.4 349.4 %window.1 = (bf16[8,128,1024]{2,1,0:T(8,128)(2,1)}, bf16[8,128,1024]{2,1,0:T(8,128)(2,1)}) custom-call(s32[16]{0:T(128)} %reshape.30.ids, f32[64]{0:T(128)} %fusion.8.coefs, bf16[128,1024]{1,0:T(8,128)(2,1)} %bitcast.6, bf16[128,1024]{1,0:T(8,128)(2,1)} %bitcast.7, bf16[8,128,1024]{2,1,0:T(8,128)(2,1)} %up_ref.1, bf16[8,128,1024]{2,1,0:T(8,128)(2,1)} %down_ref.1), custom_call_target="tpu_custom_call" | custom-call | flops 10737418240 | bytes 16777216 | tf_op jit(solution)/shard_map/window/pallas_call | solution.py:463
  353.8 0.0 copy-done
  353.8 7.6 %fusion.6 = (bf16[8,128,1024]{2,1,0:T(8,128)(2,1)}, bf16[8,128,1024]{2,1,0:T(8,128)(2,1)}, bf16[8,128,1024]{2,1,0:T(8,128)(2,1)}, bf16[8,128,1024]{2,1,0:T(8,128)(2,1)}) fusion(bf16[8,128,1024]{2,1,0:T(8,128)(2,1)} %get-tuple-element.7, bf16[8,128,1024]{2,1,0:T(8,128)(2,1)} %param.13, bf16[8,128,1024]{2,1,0:T(8,128)(2,1)} %down_ref.1, ...), kind=kLoop, calls=%fused_computation.10 | loop fusion | flops 23068672 | bytes 20971520 | tf_op jit(solution)/shard_map/convert_element_type | solution.py:512
  (3 shorter events, 0.0 us)
Async XLA Ops:
  4.4 349.4 %copy-start = (bf16[8,128,1024]{2,1,0:T(8,128)(2,1)S(1)}, bf16[8,128,1024]{2,1,0:T(8,128)(2,1)}, u32[]{:S(2)}) copy-start(bf16[8,128,1024]{2,1,0:T(8,128)(2,1)} %up_ref.1) | copy-start | bytes 6291460
